TPU v7x, 32 devices: a whole 2x2x4 slice. The times are simulated.
32 devices in a mesh: groups: 2 (over y), shard: 16 (over z, x, core).
Axes of the slice: x: 2, y: 2, z: 4, core: 2. Of those that a mesh axis runs over, the one named last changes fastest.
Arguments:
- hidden_states: bfloat16 [1024, 4096], P('groups', 'shard'), parts along dimension 0, may hold values from -6 to 6
- head_weight: bfloat16 [16384, 4096], P('shard'), may hold values from -0.09375 to 0.09375
- impact_tiles: bfloat16 [2048, 128, 128], P('shard'), may hold values from -0.23925781 to 0.23925781
- tile_active: int32 [16, 128], P('shard'), may hold values from 0 to 15, as said below
- tile_pblock: int32 [16, 128], P('shard'), may hold values from 0 to 15
- tile_count: int32 [16], P('shard'), may hold values from 1 to 128, as said below
- active_blocks: int32 [16, 16, 1], P('shard'), may hold values from 0 to 7
Outputs:
- scores: float32 [128, 32768], P('groups', 'shard'), parts along dimension 0
There are 2 independent parts, one for each index of `groups`. A program takes and returns all parts, laid end to end along the dimension named above; an argument that names none is the same for every part. Nothing has to cross between parts.
Inputs may be any that keep to these rules, and one draw needn't show every extreme that they name: Slots at or beyond tile_count of a slab are padding; the busiest slab fills all 128 slots. `tile_active`: within one slab the first min(128, 16) slots name distinct entries.
All inputs are finite; a program needn't handle non-finite values.
Results may differ from a plain program's by a relative error of at most 0.003.
Values may be sent and summed in bfloat16 or wider, within the bound.
A program may use at most 128 MiB of HBM per device.

v0:
```python
import math

import jax
import jax.numpy as jnp
from jax import lax
from jax.sharding import PartitionSpec as P

VB = 128
QLEN = 8
PB = 128
PBLK_DEV = 16


def per_device(
    hidden_states, head_weight, impact_tiles, tile_active, tile_pblock, tile_count, active_blocks
):
    token_rows = hidden_states.shape[0]
    vocab_rows = head_weight.shape[0]
    logits = lax.dot_general(
        lax.all_gather(hidden_states, "shard", axis=1, tiled=True),
        head_weight,
        (((1,), (1,)), ((), ())),
        preferred_element_type=jnp.float32,
    )
    queries = token_rows // QLEN
    pooled = jnp.max(logits.reshape(queries, QLEN, vocab_rows), axis=1)
    term_weight = jnp.log1p(jnp.maximum(pooled, 0.0)).astype(jnp.bfloat16)
    block_local = vocab_rows // VB
    blocks = jnp.transpose(term_weight.reshape(queries, block_local, VB), (1, 0, 2))
    owners = lax.axis_size("shard")
    wanted = active_blocks[0]
    everything = lax.all_gather(blocks, "shard", axis=0, tiled=True)
    offsets = jnp.arange(owners, dtype=jnp.int32)[:, None] * block_local
    table = jnp.take(everything, (offsets + wanted).reshape(-1), axis=0)
    slot_total = impact_tiles.shape[0]
    step_size = math.gcd(slot_total, 16)
    counted = tile_count[0]
    slot_entries = tile_active[0]
    slot_blocks = tile_pblock[0]
    block_ids = jnp.arange(PBLK_DEV, dtype=jnp.int32)

    def sweep_step(index, accum):
        begin = index * step_size
        entries = lax.dynamic_slice_in_dim(slot_entries, begin, step_size)
        targets = lax.dynamic_slice_in_dim(slot_blocks, begin, step_size)
        chosen = jnp.take(table, entries, axis=0)
        impacts = lax.dynamic_slice_in_dim(impact_tiles, begin, step_size, 0)
        contrib = jnp.einsum("tqv,tvp->tqp", chosen, impacts, preferred_element_type=jnp.float32)
        live = (begin + jnp.arange(step_size, dtype=jnp.int32) < counted).astype(jnp.float32)
        onehot = (targets[:, None] == block_ids[None, :]).astype(jnp.float32) * live[:, None]
        return accum + jnp.einsum("tqp,tb->qbp", contrib, onehot, precision=lax.Precision.HIGHEST)

    start_scores = jnp.zeros((queries, PBLK_DEV, PB), jnp.float32)
    trips = slot_total // step_size
    summed = lax.fori_loop(0, trips, sweep_step, start_scores)
    return summed.reshape(queries, PBLK_DEV * PB)


def solution(mesh):
    return jax.shard_map(
        per_device,
        mesh=mesh,
        in_specs=(
            P("groups", "shard"),
            P("shard", None),
            P("shard", None, None),
            P("shard", None),
            P("shard", None),
            P("shard"),
            P("shard", None, None),
        ),
        out_specs=P("groups", "shard"),
        check_vma=False,
    )
```

profile of v0, /device:TPU:0, one launch (start us, length us, event | category | flops | bytes accessed | tf_op | source)
XLA Modules:
  0.0 155.4 jit_solution(202372293380590231)
XLA Ops:
  7.3 58.1 %all-gather.3.cloned.1.call-done = bf16[512,4096]{1,0:T(8,128)(2,1)} async-done(((bf16[512,256]{1,0:T(8,128)(2,1)}), bf16[512,4096]{1,0:T(8,128)(2,1)}) %all-gather.3.cloned.1.call-update) | async-done | bytes 4194320 | tf_op jit(solution)/shard_map/all_gather | solution.py:20
  65.5 9.4 %bitcast_reduce_fusion = f32[64,1024]{1,0:T(8,128)S(1)} fusion(bf16[512,4096]{1,0:T(8,128)(2,1)} %all-gather.3.cloned.1.call-done, bf16[1024,4096]{1,0:T(8,128)(2,1)} %param.10), kind=kOutput, calls=%fused_computation.24 | convolution fusion | flops 4295426048 | bytes 12845056 | tf_op jit(solution)/shard_map/dot_general | solution.py:19
  75.8 39.7 %all-gather.5.cloned.1.call-done = bf16[128,64,128]{2,1,0:T(8,128)(2,1)} async-done(((bf16[8,64,128]{2,1,0:T(8,128)(2,1)}), bf16[128,64,128]{2,1,0:T(8,128)(2,1)}) %all-gather.5.cloned.1.call-update) | async-done | bytes 2097168 | tf_op jit(solution)/shard_map/all_gather | solution.py:32
  115.5 2.2 %gather_fusion.1 = bf16[16,64,128]{2,1,0:T(8,128)(2,1)S(1)} fusion(bf16[128,64,128]{2,1,0:T(8,128)(2,1)} %all-gather.5.cloned.1.call-done, s32[1024]{0:T(1024)S(1)} %pad_clamp_fusion.1), kind=kCustom, calls=%fused_computation.1 | custom fusion | bytes 524352 | tf_op jit(solution)/shard_map/jit(_take)/gather | solution.py:34
  117.8 29.8 %while.14 = (s32[]{:T(128)}, f32[64,16,128]{2,1,0:T(8,128)S(1)}, s32[128]{0:T(128)S(1)}, s32[]{:T(128)}, s32[128]{0:T(128)S(1)}, /*index=5*/bf16[16,64,128]{2,1,...) while((s32[]{:T(128)}, f32[64,16,128]{2,1,0:T(8,128)S(1)}, ...), condition=%wide.region_2.3_spmd.clone, body=%wide.region_1.2_spmd.clone.sunk | while | flops 59115156 | bytes 3412761 | solution.py:55
  117.8 0.7 compare_and_fusion.3
  119.2 1.4 fusion.31
  120.6 0.9 fusion.32
  121.5 0.7 compare_and_fusion.3
  122.9 1.4 fusion.31
  124.3 0.9 fusion.32
  126.6 1.4 fusion.31
  128.1 0.9 fusion.32
  130.3 1.4 fusion.31
  131.8 0.9 fusion.32
  134.1 1.4 fusion.31
  135.5 0.9 fusion.32
  137.8 1.4 fusion.31
  139.2 0.9 fusion.32
  141.5 1.4 fusion.31
  143.0 0.9 fusion.32
  145.2 1.4 fusion.31
  146.7 0.9 fusion.32
  147.6 1.0 copy.17
  (48 shorter events, 11.5 us)
Async XLA Ops:
  6.5 58.9 %all-gather.3.cloned.1.call-start = ((), (), s32[]{:S(2)}) async-start(), calls=%async_computation | async-start | bytes 4456448 | tf_op jit(solution)/shard_map/all_gather | solution.py:20
  7.3 68.5 %copy-start.1 = (s32[1,16,1]{1,2,0:T(1,128)S(1)}, s32[1,16,1]{1,2,0:T(1,128)}, u32[]{:S(2)}) copy-start(s32[1,16,1]{1,2,0:T(1,128)} %param.15) | copy-start | bytes 196
  7.3 110.5 %copy-start = (s32[1,128]{1,0:T(1,128)S(1)}, s32[1,128]{1,0:T(1,128)}, u32[]{:S(2)}) copy-start(s32[1,128]{1,0:T(1,128)} %param.12) | copy-start | bytes 1540
  7.3 110.5 %copy-start.2 = (s32[1,128]{1,0:T(1,128)S(1)}, s32[1,128]{1,0:T(1,128)}, u32[]{:S(2)}) copy-start(s32[1,128]{1,0:T(1,128)} %param.13) | copy-start | bytes 1540
  7.3 108.2 %all-gather.5.cloned.1.call-start = ((), (), s32[]{:S(2)}) async-start(), calls=%async_computation.1 | async-start | bytes 2228224 | tf_op jit(solution)/shard_map/all_gather | solution.py:32
Sparse Core Ops, SparseCore 0:
  9.5 55.9 all-gather.2
  75.9 39.5 all-gather.4
where the time goes:
time: 156 us; the launch traced here: 155 us
  waiting for transfers between devices  98.5 us (63%)
  matrix products  27.6 us (18%)
  between operations  13.5 us (9%)
  local copies, waits for them, and re-layouts  9.26 us (6%)
  other arithmetic  6.08 us (4%)
    all_gather x1, waiting for transfers between devices, per_device(): lax.all_gather(hidden_states, 'shard', axis=1, tiled=True)  58.1 us
    all_gather x1, waiting for transfers between devices, per_device(): everything = lax.all_gather(blocks, 'shard', axis=0, tiled=True)  39.7 us
    dot_general x8, matrix products, sweep_step(): jnp.einsum('tqv,tvp->tqp', chosen, impacts, preferred_element_type=jnp.fl...  10.9 us
    dot_general x1, matrix products, per_device(): lax.dot_general(lax.all_gather(hidden_states, 'shard', axis=1, tiled=True...  9.43 us
    dot_general x8, matrix products, sweep_step(): jnp.einsum('tqp,tb->qbp', contrib, onehot, precision=lax.Precision.HIGHEST)  7.3 us
    and x8, other arithmetic, sweep_step(): chosen = jnp.take(table, entries, axis=0)  5.82 us
    gather x8, local copies, waits for them, and re-layouts, sweep_step(): chosen = jnp.take(table, entries, axis=0)  4.78 us
  transfers between devices with their start and end apart: 2, of which 2 were waited for; matrix products, arithmetic and copies ran while one was open for 0% of the time, Pallas kernels for 0%

commit v1 on v0

--- a/solution.py
+++ b/solution.py
@@ -1,19 +1,314 @@
+import functools
 import math
 
 import jax
 import jax.numpy as jnp
 from jax import lax
+from jax.experimental import pallas as pl
+from jax.experimental.pallas import tpu as pltpu
 from jax.sharding import PartitionSpec as P
 
 VB = 128
 QLEN = 8
 PB = 128
 PBLK_DEV = 16
-
-
-def per_device(
-    hidden_states, head_weight, impact_tiles, tile_active, tile_pblock, tile_count, active_blocks
+MESH = pl.DeviceIdType.MESH
+
+NZ, NX, NC = 4, 2, 2
+NDEV = NZ * NX * NC
+F0, F1, G0, G1 = range(4)
+
+
+def piece_rows(rows):
+    f = rows * 9 // 32
+    g = rows // 2 - f
+    return ((0, f), (f, f), (2 * f, g), (2 * f + g, g))
+
+
+def fused_kernel(
+    rows,
+    hs_ref, w_ref, tiles_ref, act_ref, cnt_ref, ab_ref, pb_ref, out_ref,
+    hid, w_v, tiles_v, acc, tw, stage, table, pref, mine, wantv, chain_v, want_s, chain_s,
+    send_sem, recv_sem, isend, irecv, xsend, xrecv, local_sem,
 ):
+    me = lax.axis_index("shard")
+    grp = lax.axis_index("groups")
+    z, x, c = me // (NX * NC), (me // NC) % NX, me % NC
+    pieces = piece_rows(rows)
+    cols = hs_ref.shape[1]
+    vocab = w_ref.shape[0]
+    nblk = vocab // VB
+    queries = rows // QLEN
+    slots = tiles_ref.shape[0]
+
+    def at(dz, dx, dc=0):
+        return ((z + dz % NZ) % NZ) * (NX * NC) + ((x + dx) % NX) * NC + (c + dc) % NC
+
+    own_copy = pltpu.make_async_copy(hs_ref, hid.at[me], local_sem.at[0])
+    own_copy.start()
+    w_copy = pltpu.make_async_copy(w_ref, w_v, local_sem.at[1])
+    w_copy.start()
+
+    barrier = pltpu.get_barrier_semaphore()
+    for k in range(1, NDEV):
+        pl.semaphore_signal(barrier, inc=1, device_id=(grp, (me + k) % NDEV), device_id_type=MESH)
+    pl.semaphore_wait(barrier, NDEV - 1)
+
+    sends = []
+
+    def view(ref, blk, piece):
+        start, size = pieces[piece]
+        return ref.at[blk, pl.ds(start, size), :]
+
+    def send(blk, piece, to, own=False):
+        start, size = pieces[piece]
+        src = hs_ref.at[pl.ds(start, size), :] if own else view(hid, blk, piece)
+        copy = pltpu.make_async_remote_copy(
+            src_ref=src,
+            dst_ref=view(hid, blk, piece),
+            send_sem=send_sem.at[len(sends)],
+            recv_sem=recv_sem.at[blk, piece],
+            device_id=(grp, to),
+            device_id_type=MESH,
+        )
+        copy.start()
+        sends.append(copy)
+
+    def arrived(blk, piece):
+        pltpu.make_async_remote_copy(
+            src_ref=view(hid, blk, piece),
+            dst_ref=view(hid, blk, piece),
+            send_sem=send_sem.at[0],
+            recv_sem=recv_sem.at[blk, piece],
+            device_id=(grp, at(0, 0, 1)),
+            device_id_type=MESH,
+        ).wait_recv()
+
+    zp, zm, xo, sib = at(1, 0), at(-1, 0), at(0, 1), at(0, 0, 1)
+    for pz, mz, px in ((G0, G1, F0), (G1, G0, F1), (F0, F1, G0), (F1, F0, G1)):
+        send(me, pz, zp, True)
+        send(me, mz, zm, True)
+        send(me, px, xo, True)
+    for piece in range(4):
+        send(me, piece, sib, True)
+
+    tiles_copy = pltpu.make_async_copy(tiles_ref, tiles_v, local_sem.at[2])
+    tiles_copy.start()
+
+    isends = []
+    for k in range(1, NDEV):
+        owner = (me + k) % NDEV
+        mine[k] = jnp.full((8, 128), ab_ref[0, owner, 0], jnp.int32)
+        copy = pltpu.make_async_remote_copy(
+            src_ref=mine.at[k],
+            dst_ref=wantv.at[me],
+            send_sem=isend.at[k],
+            recv_sem=irecv.at[me],
+            device_id=(grp, owner),
+            device_id_type=MESH,
+        )
+        copy.start()
+        isends.append(copy)
+    wantv[me] = jnp.full((8, 128), ab_ref[0, me, 0], jnp.int32)
+
+    sub = lax.broadcasted_iota(jnp.int32, (slots, slots), 0)
+    lane = lax.broadcasted_iota(jnp.int32, (slots, slots), 1)
+    pb_row = pb_ref[...]
+    pb_col = jnp.sum(jnp.where(sub == lane, pb_row, 0), axis=1, keepdims=True)
+    live = sub < cnt_ref[0]
+    same = jnp.logical_and(jnp.logical_and(pb_col == pb_row, sub < lane), live)
+    prev = jnp.max(jnp.where(same, sub + 1, 0), axis=0, keepdims=True)
+    lasts = jnp.max(jnp.where(jnp.logical_and(pb_col == lane, live), sub + 1, 0), axis=0, keepdims=True)
+    row8 = lax.broadcasted_iota(jnp.int32, (8, slots), 0)
+    chain_v[...] = jnp.where(row8 == 0, prev, lasts)
+    chain_copy = pltpu.make_async_copy(chain_v, chain_s, local_sem.at[3])
+    chain_copy.start()
+    pref[0] = jnp.zeros((queries, PB), jnp.float32)
+
+    step_n = 256
+
+    def product(blk, n):
+        left = hid[blk]
+        right = w_v[pl.ds(pl.multiple_of(n * step_n, step_n), step_n), pl.ds(pl.multiple_of(blk * cols, cols), cols)]
+        return lax.dot_general(left, right, (((1,), (1,)), ((), ())), preferred_element_type=jnp.float32)
+
+    def multiply(blk, first=False):
+        @pl.loop(0, vocab // step_n)
+        def _(n):
+            where = pl.ds(pl.multiple_of(n * step_n, step_n), step_n)
+            if first:
+                acc[:, where] = product(blk, n)
+            else:
+                acc[:, where] += product(blk, n)
+
+    def take(blk, piece, *to):
+        arrived(blk, piece)
+        for dev in to:
+            send(blk, piece, dev)
+        send(blk, piece, sib)
+
+    def sibling(dz, dx):
+        blk = at(dz, dx, 1)
+        for piece in range(4):
+            arrived(blk, piece)
+        multiply(blk)
+
+    b_zm, b_zp, b_x, b_zz = at(-1, 0), at(1, 0), at(0, 1), at(2, 0)
+    d_zm, d_zp, d_zz = at(-1, 1), at(1, 1), at(2, 1)
+
+    take(b_zm, G0, zp, xo)
+    take(b_zp, G1, zm, xo)
+    own_copy.wait()
+    w_copy.wait()
+    multiply(me, first=True)
+    take(b_x, F0, zp, zm)
+    take(b_zm, G1, xo)
+    take(b_zp, G0, xo)
+    sibling(0, 0)
+    take(b_x, F1, zp, zm)
+    take(b_zm, F0, zp)
+    take(b_zp, F1, zm)
+    take(b_x, G0)
+    take(b_zm, F1)
+    take(b_zp, F0)
+    take(b_x, G1)
+    multiply(b_zm)
+    take(b_zz, G0, xo)
+    take(b_zz, G1, xo)
+    multiply(b_zp)
+    take(d_zm, G0)
+    take(d_zm, F0, zp)
+    take(d_zp, F1, zm)
+    multiply(b_x)
+    sibling(-1, 0)
+    take(d_zp, G1)
+    take(d_zm, G1)
+    take(d_zp, G0)
+    sibling(1, 0)
+    take(d_zm, F1)
+    take(d_zp, F0)
+    sibling(0, 1)
+    multiply(d_zm)
+    multiply(d_zp)
+
+    for k in range(1, NDEV):
+        other = (me + k) % NDEV
+        pltpu.make_async_remote_copy(
+            src_ref=mine.at[k], dst_ref=wantv.at[other], send_sem=isend.at[k],
+            recv_sem=irecv.at[other], device_id=(grp, other), device_id_type=MESH,
+        ).wait_recv()
+    want_copy = pltpu.make_async_copy(wantv, want_s, local_sem.at[4])
+    want_copy.start()
+
+    take(b_zz, F0)
+    take(b_zz, F1)
+    take(d_zz, G0)
+    take(d_zz, G1)
+    sibling(-1, 1)
+    sibling(1, 1)
+    multiply(b_zz)
+    take(d_zz, F0)
+    take(d_zz, F1)
+    sibling(2, 0)
+    multiply(d_zz)
+    want_copy.wait()
+    chain_copy.wait()
+    tiles_copy.wait()
+
+    last = at(2, 1, 1)
+    for piece in range(4):
+        arrived(last, piece)
+
+    @pl.loop(0, vocab // step_n)
+    def _(n):
+        where = pl.ds(pl.multiple_of(n * step_n, step_n), step_n)
+        total = acc[:, where] + product(last, n)
+        pooled = jnp.max(total.reshape(queries, QLEN, step_n), axis=1)
+        weight = jnp.log1p(jnp.maximum(pooled, 0.0)).astype(jnp.bfloat16)
+        for part in range(step_n // VB):
+            tw[n * (step_n // VB) + part] = weight[:, part * VB:(part + 1) * VB]
+
+    xsends = []
+    for k in range(1, NDEV):
+        slab = (me + k) % NDEV
+        stage[k] = tw[want_s[slab, 0, 0]]
+        copy = pltpu.make_async_remote_copy(
+            src_ref=stage.at[k], dst_ref=table.at[me], send_sem=xsend.at[k],
+            recv_sem=xrecv.at[me], device_id=(grp, slab), device_id_type=MESH,
+        )
+        copy.start()
+        xsends.append(copy)
+    table[me] = tw[want_s[me, 0, 0]]
+    for k in range(1, NDEV):
+        owner = (me + k) % NDEV
+        pltpu.make_async_remote_copy(
+            src_ref=stage.at[k], dst_ref=table.at[owner], send_sem=xsend.at[k],
+            recv_sem=xrecv.at[owner], device_id=(grp, owner), device_id_type=MESH,
+        ).wait_recv()
+
+    unroll = 16
+
+    @pl.loop(0, slots // unroll)
+    def _(i):
+        base = i * unroll
+        parts = []
+        for j in range(unroll):
+            t = base + j
+            parts.append(jnp.dot(table[act_ref[0, t]], tiles_v[t], preferred_element_type=jnp.float32))
+        for j in range(unroll):
+            t = base + j
+            pref[t + 1] = pref[chain_s[0, t]] + parts[j]
+
+    for b in range(PBLK_DEV):
+        out_ref[:, b * PB:(b + 1) * PB] = pref[chain_s[1, b]]
+
+    for copy in sends + isends + xsends:
+        copy.wait_send()
+
+
+def fused(hidden_states, head_weight, impact_tiles, tile_active, tile_pblock, tile_count, active_blocks):
+    rows, cols = hidden_states.shape
+    vocab, depth = head_weight.shape
+    slots = impact_tiles.shape[0]
+    queries = rows // QLEN
+    hbm = pl.BlockSpec(memory_space=pl.ANY)
+    smem = pl.BlockSpec(memory_space=pltpu.SMEM)
+    vmem = pl.BlockSpec(memory_space=pltpu.VMEM)
+    return pl.pallas_call(
+        functools.partial(fused_kernel, rows),
+        out_shape=jax.ShapeDtypeStruct((queries, PBLK_DEV * PB), jnp.float32),
+        in_specs=[hbm, hbm, hbm, smem, smem, smem, vmem],
+        out_specs=vmem,
+        scratch_shapes=[
+            pltpu.VMEM((NDEV, rows, cols), jnp.bfloat16),
+            pltpu.VMEM((vocab, depth), jnp.bfloat16),
+            pltpu.VMEM((slots, VB, PB), jnp.bfloat16),
+            pltpu.VMEM((rows, vocab), jnp.float32),
+            pltpu.VMEM((vocab // VB, queries, VB), jnp.bfloat16),
+            pltpu.VMEM((NDEV, queries, VB), jnp.bfloat16),
+            pltpu.VMEM((NDEV, queries, VB), jnp.bfloat16),
+            pltpu.VMEM((slots + 1, queries, PB), jnp.float32),
+            pltpu.VMEM((NDEV, 8, 128), jnp.int32),
+            pltpu.VMEM((NDEV, 8, 128), jnp.int32),
+            pltpu.VMEM((8, slots), jnp.int32),
+            pltpu.SMEM((NDEV, 8, 128), jnp.int32),
+            pltpu.SMEM((8, slots), jnp.int32),
+            pltpu.SemaphoreType.DMA((64,)),
+            pltpu.SemaphoreType.DMA((NDEV, 4)),
+            pltpu.SemaphoreType.DMA((NDEV,)),
+            pltpu.SemaphoreType.DMA((NDEV,)),
+            pltpu.SemaphoreType.DMA((NDEV,)),
+            pltpu.SemaphoreType.DMA((NDEV,)),
+            pltpu.SemaphoreType.DMA((5,)),
+        ],
+        compiler_params=pltpu.CompilerParams(
+            collective_id=0, has_side_effects=True, vmem_limit_bytes=44 * 1024 * 1024
+        ),
+        name="encode_and_score",
+    )(hidden_states, head_weight, impact_tiles, tile_active, tile_count, active_blocks, tile_pblock)
+
+
+def general(hidden_states, head_weight, impact_tiles, tile_active, tile_pblock, tile_count, active_blocks):
     token_rows = hidden_states.shape[0]
     vocab_rows = head_weight.shape[0]
     logits = lax.dot_general(
@@ -56,6 +351,20 @@
     return summed.reshape(queries, PBLK_DEV * PB)
 
 
+def per_device(hidden_states, head_weight, impact_tiles, tile_active, tile_pblock, tile_count, active_blocks):
+    rows, cols = hidden_states.shape
+    fits = (
+        lax.axis_size("shard") == NDEV
+        and rows == 512
+        and cols % 128 == 0
+        and head_weight.shape[0] % 256 == 0
+        and impact_tiles.shape[0] == 128
+        and active_blocks.shape[2] == 1
+    )
+    run = fused if fits else general
+    return run(hidden_states, head_weight, impact_tiles, tile_active, tile_pblock, tile_count, active_blocks)
+
+
 def solution(mesh):
     return jax.shard_map(
         per_device,

time: 156 us -> 60.7 us (0.39)
  the two profiles are of different devices: /device:TPU:0 before, /device:TPU:27 now
where the time goes in v1:
time: 60.7 us; the launch traced here: 60.5 us
  Pallas kernels  53.8 us (89%)
  local copies, waits for them, and re-layouts  5.97 us (10%)
  between operations  0.67 us (1%)
    pallas_call x1, Pallas kernels, fused(): pl.pallas_call(functools.partial(fused_kernel, rows), out_shape=jax.Shape...  53.8 us
    unnamed x10, local copies, waits for them, and re-layouts  5.97 us

profile of v1, /device:TPU:27, one launch (start us, length us, event | category | flops | bytes accessed | tf_op | source)
XLA Modules:
  0.0 60.5 jit_solution(9699583645189040730)
XLA Ops:
  0.7 0.7 %copy.8.ab_ref = s32[1,16,1]{2,1,0:T(8,128)S(1)} copy(s32[1,16,1]{1,2,0:T(1,128)} %param.13) | data formatting | bytes 128 | tf_op args[6]
  1.4 0.0 copy-start
  1.4 2.2 %copy-done = bf16[128,128,128]{2,1,0:T(8,128)(2,1)S(1)} copy-done((bf16[128,128,128]{2,1,0:T(8,128)(2,1)S(1)}, bf16[128,128,128]{2,1,0:T(8,128)(2,1)}, u32[]{:S(2)}) %copy-start) | copy-done | bytes 4194328
  3.6 0.0 copy-start.1
  3.6 0.9 %copy-done.1 = bf16[512,256]{1,0:T(8,128)(2,1)S(1)} copy-done((bf16[512,256]{1,0:T(8,128)(2,1)S(1)}, bf16[512,256]{1,0:T(8,128)(2,1)}, u32[]{:S(2)}) %copy-start.1) | copy-done | bytes 262168
  4.5 0.0 copy-start.2
  4.5 0.7 %copy-done.2 = s32[1,128]{1,0:T(1,128)S(1)} copy-done((s32[1,128]{1,0:T(1,128)S(1)}, s32[1,128]{1,0:T(1,128)}, u32[]{:S(2)}) %copy-start.2) | copy-done | bytes 536
  5.2 0.0 copy-start.3
  5.2 0.7 %copy-done.3 = s32[1,128]{1,0:T(1,128)S(1)} copy-done((s32[1,128]{1,0:T(1,128)S(1)}, s32[1,128]{1,0:T(1,128)}, u32[]{:S(2)}) %copy-start.3) | copy-done | bytes 536
  5.8 53.8 %encode_and_score.1 = f32[64,2048]{1,0:T(8,128)S(1)} custom-call(bf16[512,256]{1,0:T(8,128)(2,1)S(1)} %copy-done.1, bf16[1024,4096]{1,0:T(8,128)(2,1)} %w_ref.1, bf16[128,128,128]{2,1,0:T(8,128)(2,1)S(1)} %copy-done, s32[1,128]{1,0:T(1,128)S(1)} %copy-done.2, s32[1]{0:T(128)S(6)} %copy.10.cnt_ref, s32[1,16,1]{2,1,0:T(8,128)S(1)} %copy.8.ab_ref, ...), custom_call_target="tpu_custom_call" | custom-call | tf_op jit(solution)/shard_map/encode_and_score/pallas_call | solution.py:277
  59.7 0.8 %copy.11 = f32[64,2048]{1,0:T(8,128)} copy(f32[64,2048]{1,0:T(8,128)S(1)} %encode_and_score.1) | data formatting | bytes 1048576
Async XLA Ops:
  1.4 2.2 %copy-start = (bf16[128,128,128]{2,1,0:T(8,128)(2,1)S(1)}, bf16[128,128,128]{2,1,0:T(8,128)(2,1)}, u32[]{:S(2)}) copy-start(bf16[128,128,128]{2,1,0:T(8,128)(2,1)} %tiles_ref.1) | copy-start | bytes 12582916
  3.6 0.9 %copy-start.1 = (bf16[512,256]{1,0:T(8,128)(2,1)S(1)}, bf16[512,256]{1,0:T(8,128)(2,1)}, u32[]{:S(2)}) copy-start(bf16[512,256]{1,0:T(8,128)(2,1)} %hs_ref.1) | copy-start | bytes 786436
  4.5 0.7 %copy-start.2 = (s32[1,128]{1,0:T(1,128)S(1)}, s32[1,128]{1,0:T(1,128)}, u32[]{:S(2)}) copy-start(s32[1,128]{1,0:T(1,128)} %act_ref.1) | copy-start | bytes 1540
  5.2 0.7 %copy-start.3 = (s32[1,128]{1,0:T(1,128)S(1)}, s32[1,128]{1,0:T(1,128)}, u32[]{:S(2)}) copy-start(s32[1,128]{1,0:T(1,128)} %pb_ref.1) | copy-start | bytes 1540

commit v2 on v0

--- a/solution.py
+++ b/solution.py
@@ -3,17 +3,385 @@
 import jax
 import jax.numpy as jnp
 from jax import lax
+from jax.experimental import pallas as pl
+from jax.experimental.pallas import tpu as pltpu
 from jax.sharding import PartitionSpec as P
 
 VB = 128
 QLEN = 8
 PB = 128
 PBLK_DEV = 16
-
-
-def per_device(
-    hidden_states, head_weight, impact_tiles, tile_active, tile_pblock, tile_count, active_blocks
+MESH = pl.DeviceIdType.MESH
+
+NZ, NX, NC = 4, 2, 2
+NDEV = NZ * NX * NC
+GROUPS = ((80, 144, 144, 144),)
+GROUP_ROWS = sum(GROUPS[0])
+PIECES = []
+for sizes in GROUPS:
+    PIECES.append([])
+    for size in sizes:
+        done = sum(n for group in PIECES for _, n in group)
+        PIECES[-1].append((done, size))
+NPIECE = len(GROUPS[0])
+NSEND = 128
+
+
+def fused_kernel(
+    hs_ref, w_ref, tiles_ref, act_hbm, cnt_hbm, ab_hbm, pb_hbm, out_ref,
+    hid, w_v, tiles_v, acc, tw, stage, table, pref, mine, wantv, chain_v, want_s, chain_s,
+    act_ref, cnt_ref, ab_ref, pb_ref, send_sem, recv_sem, isend, irecv, xsend, xrecv, local_sem,
 ):
+    me = lax.axis_index("shard")
+    grp = lax.axis_index("groups")
+    z, x, c = me // (NX * NC), (me // NC) % NX, me % NC
+    cols = hs_ref.shape[1]
+    vocab = w_ref.shape[0]
+    nblk = vocab // VB
+    gq = GROUP_ROWS // QLEN
+    slots = tiles_ref.shape[0]
+
+    def at(zz, dx, dc=0):
+        return zz * (NX * NC) + ((x + dx) % NX) * NC + (c + dc) % NC
+
+    small = [
+        pltpu.make_async_copy(src, dst, local_sem.at[5 + i])
+        for i, (src, dst) in enumerate(
+            ((ab_hbm, ab_ref), (pb_hbm, pb_ref), (cnt_hbm, cnt_ref), (act_hbm, act_ref))
+        )
+    ]
+    for copy in small:
+        copy.start()
+    own_copy = pltpu.make_async_copy(hs_ref, hid.at[me], local_sem.at[0])
+    own_copy.start()
+    w_copy = pltpu.make_async_copy(w_ref, w_v, local_sem.at[1])
+    w_copy.start()
+
+    barrier = pltpu.get_barrier_semaphore()
+    for k in range(1, NDEV):
+        pl.semaphore_signal(barrier, inc=1, device_id=(grp, (me + k) % NDEV), device_id_type=MESH)
+    pl.semaphore_wait(barrier, NDEV - 1)
+
+    sends = []
+    isends = []
+    has_up, has_down = z < NZ - 1, z > 0
+    middle = jnp.logical_and(has_up, has_down)
+    up, down = jnp.minimum(z + 1, NZ - 1), jnp.maximum(z - 1, 0)
+    xo, sib = at(z, 1), at(z, 0, 1)
+
+    def view(ref, blk, g, p):
+        start, size = PIECES[g][p]
+        return ref.at[blk, pl.ds(start, size), :]
+
+    def send(blk, g, p, to, own=False, when=None):
+        start, size = PIECES[g][p]
+        copy = pltpu.make_async_remote_copy(
+            src_ref=hs_ref.at[pl.ds(start, size), :] if own else view(hid, blk, g, p),
+            dst_ref=view(hid, blk, g, p),
+            send_sem=send_sem.at[len(sends)],
+            recv_sem=recv_sem.at[blk, g * NPIECE + p],
+            device_id=(grp, to),
+            device_id_type=MESH,
+        )
+        sends.append((when, copy))
+        if when is None:
+            copy.start()
+        else:
+            pl.when(when)(copy.start)
+
+    def arrived(blk, g, p):
+        pltpu.make_async_remote_copy(
+            src_ref=view(hid, blk, g, p),
+            dst_ref=view(hid, blk, g, p),
+            send_sem=send_sem.at[0],
+            recv_sem=recv_sem.at[blk, g * NPIECE + p],
+            device_id=(grp, sib),
+            device_id_type=MESH,
+        ).wait_recv()
+
+    flip = z >= NZ // 2
+    folded = jnp.where(flip, NZ - 1 - z, z)
+
+    def near(j):
+        n = jnp.where(folded > j, j, j + 1)
+        return jnp.where(flip, NZ - 1 - n, n)
+
+    nears = [near(j) for j in range(NZ - 1)]
+    F, GS = 0, range(1, NPIECE)
+
+    def send_own(g):
+        send(me, g, F, xo, own=True)
+        for p in GS:
+            send(me, g, p, at(up, 0), own=True, when=has_up)
+            send(me, g, p, at(down, 0), own=True, when=has_down)
+            send(me, g, p, xo, own=True)
+        send(me, g, F, at(up, 0), own=True, when=has_up)
+        send(me, g, F, at(down, 0), own=True, when=has_down)
+        for p in range(NPIECE):
+            send(me, g, p, sib, own=True)
+
+    def onward(zz, dx):
+        return at(jnp.where(zz < z, up, down), dx)
+
+    def take_column(g, zz):
+        blk = at(zz, 0)
+        for p in (*GS, F):
+            arrived(blk, g, p)
+            send(blk, g, p, onward(zz, 0), when=middle)
+            if p != F:
+                send(blk, g, p, xo)
+            send(blk, g, p, sib)
+
+    def take_partner(g):
+        blk = at(z, 1)
+        arrived(blk, g, F)
+        send(blk, g, F, at(up, 0), when=has_up)
+        send(blk, g, F, at(down, 0), when=has_down)
+        send(blk, g, F, sib)
+        for p in GS:
+            arrived(blk, g, p)
+            send(blk, g, p, sib)
+
+    def take_cross_f(g, zz):
+        blk = at(zz, 1)
+        arrived(blk, g, F)
+        send(blk, g, F, onward(zz, 0), when=middle)
+        send(blk, g, F, sib)
+
+    def take_cross_g(g, zz):
+        blk = at(zz, 1)
+        for p in GS:
+            arrived(blk, g, p)
+            send(blk, g, p, sib)
+
+    step_n = 512
+
+    def product(g, chip, n):
+        total = None
+        for core in range(NC):
+            blk = chip * NC + core
+            left = hid[blk, g * GROUP_ROWS:(g + 1) * GROUP_ROWS, :]
+            right = w_v[pl.ds(pl.multiple_of(n * step_n, step_n), step_n), pl.ds(pl.multiple_of(blk * cols, cols), cols)]
+            part = lax.dot_general(left, right, (((1,), (1,)), ((), ())), preferred_element_type=jnp.float32)
+            total = part if total is None else total + part
+        return total
+
+    def wait_sibling(g, zz, dx):
+        for p in range(NPIECE):
+            arrived(at(zz, dx, 1), g, p)
+        return zz * NX + (x + dx) % NX
+
+    def multiply(g, zz, dx, first=False):
+        chip = wait_sibling(g, zz, dx)
+
+        @pl.loop(0, vocab // step_n)
+        def _(n):
+            where = pl.ds(pl.multiple_of(n * step_n, step_n), step_n)
+            if first:
+                acc[g, :, where] = product(g, chip, n)
+            else:
+                acc[g, :, where] += product(g, chip, n)
+
+    def multiply_last(g, zz, dx):
+        chip = wait_sibling(g, zz, dx)
+
+        @pl.loop(0, vocab // step_n)
+        def _(n):
+            where = pl.ds(pl.multiple_of(n * step_n, step_n), step_n)
+            total = acc[g, :, where] + product(g, chip, n)
+            pooled = jnp.max(total.reshape(gq, QLEN, step_n), axis=1)
+            weight = jnp.log1p(jnp.maximum(pooled, 0.0)).astype(jnp.bfloat16)
+            for part in range(step_n // VB):
+                tw[g, n * (step_n // VB) + part] = weight[:, part * VB:(part + 1) * VB]
+
+    def send_weights(g):
+        for k in range(1, NDEV):
+            slab = (me + k) % NDEV
+            stage[g, k] = tw[g, want_s[slab, 0, 0]]
+            copy = pltpu.make_async_remote_copy(
+                src_ref=stage.at[g, k], dst_ref=table.at[g, me], send_sem=xsend.at[g, k],
+                recv_sem=xrecv.at[g, me], device_id=(grp, slab), device_id_type=MESH,
+            )
+            copy.start()
+            isends.append(copy)
+        table[g, me] = tw[g, want_s[me, 0, 0]]
+
+    unroll = 16
+
+    def score(g):
+        for k in range(1, NDEV):
+            owner = (me + k) % NDEV
+            pltpu.make_async_remote_copy(
+                src_ref=stage.at[g, k], dst_ref=table.at[g, owner], send_sem=xsend.at[g, k],
+                recv_sem=xrecv.at[g, owner], device_id=(grp, owner), device_id_type=MESH,
+            ).wait_recv()
+
+        @pl.loop(0, slots // unroll)
+        def _(i):
+            base = i * unroll
+            parts = []
+            for j in range(unroll):
+                t = base + j
+                parts.append(jnp.dot(table[g, act_ref[0, t]], tiles_v[t], preferred_element_type=jnp.float32))
+            for j in range(unroll):
+                t = base + j
+                pref[t + 1] = pref[chain_s[0, t]] + parts[j]
+
+        for b in range(PBLK_DEV):
+            out_ref[g * gq:(g + 1) * gq, b * PB:(b + 1) * PB] = pref[chain_s[1, b]]
+
+    send_own(0)
+    tiles_copy = pltpu.make_async_copy(tiles_ref, tiles_v, local_sem.at[2])
+    tiles_copy.start()
+    for copy in small:
+        copy.wait()
+
+    for k in range(1, NDEV):
+        owner = (me + k) % NDEV
+        mine[k] = jnp.full((1, 128), ab_ref[0, owner], jnp.int32)
+        copy = pltpu.make_async_remote_copy(
+            src_ref=mine.at[k],
+            dst_ref=wantv.at[me],
+            send_sem=isend.at[k],
+            recv_sem=irecv.at[me],
+            device_id=(grp, owner),
+            device_id_type=MESH,
+        )
+        copy.start()
+        isends.append(copy)
+    wantv[me] = jnp.full((1, 128), ab_ref[0, me], jnp.int32)
+
+    sub = lax.broadcasted_iota(jnp.int32, (slots, slots), 0)
+    lane = lax.broadcasted_iota(jnp.int32, (slots, slots), 1)
+    pb_row = pb_ref[...]
+    pb_col = jnp.sum(jnp.where(sub == lane, pb_row, 0), axis=1, keepdims=True)
+    live = sub < cnt_ref[0, 0]
+    same = jnp.logical_and(jnp.logical_and(pb_col == pb_row, sub < lane), live)
+    prev = jnp.max(jnp.where(same, sub + 1, 0), axis=0, keepdims=True)
+    lasts = jnp.max(jnp.where(jnp.logical_and(pb_col == lane, live), sub + 1, 0), axis=0, keepdims=True)
+    row8 = lax.broadcasted_iota(jnp.int32, (8, slots), 0)
+    chain_v[...] = jnp.where(row8 == 0, prev, lasts)
+    chain_copy = pltpu.make_async_copy(chain_v, chain_s, local_sem.at[3])
+    chain_copy.start()
+    pref[0] = jnp.zeros((gq, PB), jnp.float32)
+    own_copy.wait()
+    w_copy.wait()
+
+    def opening(g):
+        take_column(g, nears[0])
+        take_partner(g)
+
+    def middle_part(g):
+        multiply(g, z, 0, first=True)
+        take_column(g, nears[1])
+        take_cross_f(g, nears[0])
+        multiply(g, nears[0], 0)
+        multiply(g, z, 1)
+        take_cross_g(g, nears[0])
+
+    def closing(g):
+        take_column(g, nears[2])
+        take_cross_f(g, nears[1])
+        multiply(g, nears[1], 0)
+        multiply(g, nears[0], 1)
+        take_cross_g(g, nears[1])
+        take_cross_f(g, nears[2])
+        multiply(g, nears[2], 0)
+        multiply(g, nears[1], 1)
+        take_cross_g(g, nears[2])
+
+    def weights(g):
+        multiply_last(g, nears[2], 1)
+        send_weights(g)
+
+    def fetch_wants():
+        for k in range(1, NDEV):
+            other = (me + k) % NDEV
+            pltpu.make_async_remote_copy(
+                src_ref=mine.at[k], dst_ref=wantv.at[other], send_sem=isend.at[k],
+                recv_sem=irecv.at[other], device_id=(grp, other), device_id_type=MESH,
+            ).wait_recv()
+        want_copy = pltpu.make_async_copy(wantv, want_s, local_sem.at[4])
+        want_copy.start()
+        want_copy.wait()
+
+    ngroup = len(GROUPS)
+    opening(0)
+    for g in range(ngroup):
+        more = g + 1 < ngroup
+        if more:
+            send_own(g + 1)
+        middle_part(g)
+        if g == 0:
+            fetch_wants()
+        if more:
+            opening(g + 1)
+        closing(g)
+        weights(g)
+    chain_copy.wait()
+    tiles_copy.wait()
+    for g in range(ngroup):
+        score(g)
+
+    for when, copy in sends:
+        if when is None:
+            copy.wait_send()
+        else:
+            pl.when(when)(copy.wait_send)
+    for copy in isends:
+        copy.wait_send()
+
+
+def fused(hidden_states, head_weight, impact_tiles, tile_active, tile_pblock, tile_count, active_blocks):
+    rows, cols = hidden_states.shape
+    vocab, depth = head_weight.shape
+    slots = impact_tiles.shape[0]
+    queries = rows // QLEN
+    ngroup, gq = len(GROUPS), GROUP_ROWS // QLEN
+    hbm = pl.BlockSpec(memory_space=pl.ANY)
+    vmem = pl.BlockSpec(memory_space=pltpu.VMEM)
+    return pl.pallas_call(
+        fused_kernel,
+        out_shape=jax.ShapeDtypeStruct((queries, PBLK_DEV * PB), jnp.float32),
+        in_specs=[hbm] * 7,
+        out_specs=vmem,
+        scratch_shapes=[
+            pltpu.VMEM((NDEV, rows, cols), jnp.bfloat16),
+            pltpu.VMEM((vocab, depth), jnp.bfloat16),
+            pltpu.VMEM((slots, VB, PB), jnp.bfloat16),
+            pltpu.VMEM((ngroup, GROUP_ROWS, vocab), jnp.float32),
+            pltpu.VMEM((ngroup, vocab // VB, gq, VB), jnp.bfloat16),
+            pltpu.VMEM((ngroup, NDEV, gq, VB), jnp.bfloat16),
+            pltpu.VMEM((ngroup, NDEV, gq, VB), jnp.bfloat16),
+            pltpu.VMEM((slots + 1, gq, PB), jnp.float32),
+            pltpu.VMEM((NDEV, 1, 128), jnp.int32),
+            pltpu.VMEM((NDEV, 1, 128), jnp.int32),
+            pltpu.VMEM((8, slots), jnp.int32),
+            pltpu.SMEM((NDEV, 1, 128), jnp.int32),
+            pltpu.SMEM((8, slots), jnp.int32),
+            pltpu.SMEM((1, slots), jnp.int32),
+            pltpu.SMEM((1, 1), jnp.int32),
+            pltpu.SMEM((1, NDEV), jnp.int32),
+            pltpu.VMEM((1, slots), jnp.int32),
+            pltpu.SemaphoreType.DMA((NSEND,)),
+            pltpu.SemaphoreType.DMA((NDEV, ngroup * NPIECE)),
+            pltpu.SemaphoreType.DMA((NDEV,)),
+            pltpu.SemaphoreType.DMA((NDEV,)),
+            pltpu.SemaphoreType.DMA((ngroup, NDEV)),
+            pltpu.SemaphoreType.DMA((ngroup, NDEV)),
+            pltpu.SemaphoreType.DMA((9,)),
+        ],
+        compiler_params=pltpu.CompilerParams(
+            collective_id=0, has_side_effects=True, vmem_limit_bytes=60 * 1024 * 1024
+        ),
+        name="encode_and_score",
+    )(
+        hidden_states, head_weight, impact_tiles, tile_active, tile_count.reshape(1, 1),
+        active_blocks.reshape(1, NDEV), tile_pblock,
+    )
+
+
+def general(hidden_states, head_weight, impact_tiles, tile_active, tile_pblock, tile_count, active_blocks):
     token_rows = hidden_states.shape[0]
     vocab_rows = head_weight.shape[0]
     logits = lax.dot_general(
@@ -56,6 +424,20 @@
     return summed.reshape(queries, PBLK_DEV * PB)
 
 
+def per_device(hidden_states, head_weight, impact_tiles, tile_active, tile_pblock, tile_count, active_blocks):
+    rows, cols = hidden_states.shape
+    fits = (
+        lax.axis_size("shard") == NDEV
+        and rows == len(GROUPS) * GROUP_ROWS
+        and cols % 128 == 0
+        and head_weight.shape[0] % 256 == 0
+        and impact_tiles.shape[0] == 128
+        and active_blocks.shape[2] == 1
+    )
+    run = fused if fits else general
+    return run(hidden_states, head_weight, impact_tiles, tile_active, tile_pblock, tile_count, active_blocks)
+
+
 def solution(mesh):
     return jax.shard_map(
         per_device,

time: 156 us -> 48.9 us (0.31)
  the two profiles are of different devices: /device:TPU:0 before, /device:TPU:27 now
where the time goes in v2:
time: 48.9 us; the launch traced here: 48.8 us
  Pallas kernels  46.2 us (94%)
  local copies, waits for them, and re-layouts  1.87 us (4%)
  between operations  0.66 us (1%)
    pallas_call x1, Pallas kernels, fused(): pl.pallas_call(fused_kernel, out_shape=jax.ShapeDtypeStruct((queries, PBL...  46.2 us
    unnamed x1, local copies, waits for them, and re-layouts  1.87 us

profile of v2, /device:TPU:27, one launch (start us, length us, event | category | flops | bytes accessed | tf_op | source)
XLA Modules:
  0.0 48.8 jit_solution(5581999682073029876)
XLA Ops:
  0.7 46.2 %encode_and_score.1 = f32[64,2048]{1,0:T(8,128)} custom-call(bf16[512,256]{1,0:T(8,128)(2,1)} %hs_ref.1, bf16[1024,4096]{1,0:T(8,128)(2,1)} %w_ref.1, bf16[128,128,128]{2,1,0:T(8,128)(2,1)} %tiles_ref.1, s32[1,128]{1,0:T(1,128)} %act_hbm.1, s32[1,1]{1,0:T(1,128)} %bitcast.2.cnt_hbm, s32[1,16]{1,0:T(1,128)} %bitcast.3, s32[1,128]{1,0:T(1,128)} %pb_hbm.1), custom_call_target="tpu_custom_call" | custom-call | tf_op jit(solution)/shard_map/encode_and_score/pallas_call | solution.py:343
  46.9 1.9 %copy.10 = f32[64,2048]{1,0:T(8,128)} copy(f32[64,2048]{1,0:T(8,128)} %encode_and_score.1) | data formatting | bytes 1048576

commit v3 on v2

--- a/solution.py
+++ b/solution.py
@@ -154,14 +154,14 @@
             arrived(blk, g, p)
             send(blk, g, p, sib)
 
-    step_n = 512
+    step_n = math.gcd(vocab, 1024)
 
     def product(g, chip, n):
         total = None
         for core in range(NC):
             blk = chip * NC + core
             left = hid[blk, g * GROUP_ROWS:(g + 1) * GROUP_ROWS, :]
-            right = w_v[pl.ds(pl.multiple_of(n * step_n, step_n), step_n), pl.ds(pl.multiple_of(blk * cols, cols), cols)]
+            right = w_v[n * step_n:(n + 1) * step_n, pl.ds(pl.multiple_of(blk * cols, cols), cols)]
             part = lax.dot_general(left, right, (((1,), (1,)), ((), ())), preferred_element_type=jnp.float32)
             total = part if total is None else total + part
         return total
@@ -174,9 +174,8 @@
     def multiply(g, zz, dx, first=False):
         chip = wait_sibling(g, zz, dx)
 
-        @pl.loop(0, vocab // step_n)
-        def _(n):
-            where = pl.ds(pl.multiple_of(n * step_n, step_n), step_n)
+        for n in range(vocab // step_n):
+            where = slice(n * step_n, (n + 1) * step_n)
             if first:
                 acc[g, :, where] = product(g, chip, n)
             else:
@@ -185,9 +184,8 @@
     def multiply_last(g, zz, dx):
         chip = wait_sibling(g, zz, dx)
 
-        @pl.loop(0, vocab // step_n)
-        def _(n):
-            where = pl.ds(pl.multiple_of(n * step_n, step_n), step_n)
+        for n in range(vocab // step_n):
+            where = slice(n * step_n, (n + 1) * step_n)
             total = acc[g, :, where] + product(g, chip, n)
             pooled = jnp.max(total.reshape(gq, QLEN, step_n), axis=1)
             weight = jnp.log1p(jnp.maximum(pooled, 0.0)).astype(jnp.bfloat16)
@@ -231,8 +229,6 @@
             out_ref[g * gq:(g + 1) * gq, b * PB:(b + 1) * PB] = pref[chain_s[1, b]]
 
     send_own(0)
-    tiles_copy = pltpu.make_async_copy(tiles_ref, tiles_v, local_sem.at[2])
-    tiles_copy.start()
     for copy in small:
         copy.wait()
 
@@ -264,8 +260,6 @@
     chain_copy = pltpu.make_async_copy(chain_v, chain_s, local_sem.at[3])
     chain_copy.start()
     pref[0] = jnp.zeros((gq, PB), jnp.float32)
-    own_copy.wait()
-    w_copy.wait()
 
     def opening(g):
         take_column(g, nears[0])
@@ -307,6 +301,10 @@
 
     ngroup = len(GROUPS)
     opening(0)
+    own_copy.wait()
+    w_copy.wait()
+    tiles_copy = pltpu.make_async_copy(tiles_ref, tiles_v, local_sem.at[2])
+    tiles_copy.start()
     for g in range(ngroup):
         more = g + 1 < ngroup
         if more:

time: 48.9 us -> 47.1 us (0.963)
  Pallas kernels: 46.2 us -> 44.4 us
    pallas_call x1, Pallas kernels: 46.2 us -> 44.4 us  [fused(): pl.pallas_call(fused_kernel, out_shape=jax.ShapeDtypeStruct((queries, PBL...]
where the time goes in v3:
time: 47.1 us; the launch traced here: 46.9 us
  Pallas kernels  44.4 us (94%)
  local copies, waits for them, and re-layouts  1.87 us (4%)
  between operations  0.66 us (1%)
    pallas_call x1, Pallas kernels, fused(): pl.pallas_call(fused_kernel, out_shape=jax.ShapeDtypeStruct((queries, PBL...  44.4 us
    unnamed x1, local copies, waits for them, and re-layouts  1.87 us

profile of v3, /device:TPU:27, one launch (start us, length us, event | category | flops | bytes accessed | tf_op | source)
XLA Modules:
  0.0 46.9 jit_solution(10619771734945575321)
XLA Ops:
  0.7 44.4 %encode_and_score.1 = f32[64,2048]{1,0:T(8,128)} custom-call(bf16[512,256]{1,0:T(8,128)(2,1)} %hs_ref.1, bf16[1024,4096]{1,0:T(8,128)(2,1)} %w_ref.1, bf16[128,128,128]{2,1,0:T(8,128)(2,1)} %tiles_ref.1, s32[1,128]{1,0:T(1,128)} %act_hbm.1, s32[1,1]{1,0:T(1,128)} %bitcast.2.cnt_hbm, s32[1,16]{1,0:T(1,128)} %bitcast.3, s32[1,128]{1,0:T(1,128)} %pb_hbm.1), custom_call_target="tpu_custom_call" | custom-call | tf_op jit(solution)/shard_map/encode_and_score/pallas_call | solution.py:341
  45.0 1.9 %copy.10 = f32[64,2048]{1,0:T(8,128)} copy(f32[64,2048]{1,0:T(8,128)} %encode_and_score.1) | data formatting | bytes 1048576

commit v4 on v3

--- a/solution.py
+++ b/solution.py
@@ -30,7 +30,7 @@
 def fused_kernel(
     hs_ref, w_ref, tiles_ref, act_hbm, cnt_hbm, ab_hbm, pb_hbm, out_ref,
     hid, w_v, tiles_v, acc, tw, stage, table, pref, mine, wantv, chain_v, want_s, chain_s,
-    act_ref, cnt_ref, ab_ref, pb_ref, send_sem, recv_sem, isend, irecv, xsend, xrecv, local_sem,
+    act_ref, cnt_ref, ab_ref, pb_ref, out_v, send_sem, recv_sem, isend, irecv, xsend, xrecv, local_sem,
 ):
     me = lax.axis_index("shard")
     grp = lax.axis_index("groups")
@@ -205,6 +205,7 @@
         table[g, me] = tw[g, want_s[me, 0, 0]]
 
     unroll = 16
+    outs = []
 
     def score(g):
         for k in range(1, NDEV):
@@ -226,7 +227,12 @@
                 pref[t + 1] = pref[chain_s[0, t]] + parts[j]
 
         for b in range(PBLK_DEV):
-            out_ref[g * gq:(g + 1) * gq, b * PB:(b + 1) * PB] = pref[chain_s[1, b]]
+            out_v[b] = pref[chain_s[1, b]]
+            if b % 4 == 3:
+                part = pl.ds(b - 3, 4)
+                copy = pltpu.make_async_copy(out_v.at[part], out_ref.at[part], local_sem.at[9 + b // 4])
+                copy.start()
+                outs.append(copy)
 
     send_own(0)
     for copy in small:
@@ -328,6 +334,8 @@
             pl.when(when)(copy.wait_send)
     for copy in isends:
         copy.wait_send()
+    for copy in outs:
+        copy.wait()
 
 
 def fused(hidden_states, head_weight, impact_tiles, tile_active, tile_pblock, tile_count, active_blocks):
@@ -337,12 +345,11 @@
     queries = rows // QLEN
     ngroup, gq = len(GROUPS), GROUP_ROWS // QLEN
     hbm = pl.BlockSpec(memory_space=pl.ANY)
-    vmem = pl.BlockSpec(memory_space=pltpu.VMEM)
-    return pl.pallas_call(
+    scores = pl.pallas_call(
         fused_kernel,
-        out_shape=jax.ShapeDtypeStruct((queries, PBLK_DEV * PB), jnp.float32),
+        out_shape=jax.ShapeDtypeStruct((PBLK_DEV, queries, PB), jnp.float32),
         in_specs=[hbm] * 7,
-        out_specs=vmem,
+        out_specs=hbm,
         scratch_shapes=[
             pltpu.VMEM((NDEV, rows, cols), jnp.bfloat16),
             pltpu.VMEM((vocab, depth), jnp.bfloat16),
@@ -361,13 +368,14 @@
             pltpu.SMEM((1, 1), jnp.int32),
             pltpu.SMEM((1, NDEV), jnp.int32),
             pltpu.VMEM((1, slots), jnp.int32),
+            pltpu.VMEM((PBLK_DEV, queries, PB), jnp.float32),
             pltpu.SemaphoreType.DMA((NSEND,)),
             pltpu.SemaphoreType.DMA((NDEV, ngroup * NPIECE)),
             pltpu.SemaphoreType.DMA((NDEV,)),
             pltpu.SemaphoreType.DMA((NDEV,)),
             pltpu.SemaphoreType.DMA((ngroup, NDEV)),
             pltpu.SemaphoreType.DMA((ngroup, NDEV)),
-            pltpu.SemaphoreType.DMA((9,)),
+            pltpu.SemaphoreType.DMA((13,)),
         ],
         compiler_params=pltpu.CompilerParams(
             collective_id=0, has_side_effects=True, vmem_limit_bytes=60 * 1024 * 1024
@@ -377,6 +385,7 @@
         hidden_states, head_weight, impact_tiles, tile_active, tile_count.reshape(1, 1),
         active_blocks.reshape(1, NDEV), tile_pblock,
     )
+    return jnp.transpose(scores, (1, 0, 2)).reshape(queries, PBLK_DEV * PB)
 
 
 def general(hidden_states, head_weight, impact_tiles, tile_active, tile_pblock, tile_count, active_blocks):

time: 47.1 us -> 46.9 us (level)
    unnamed x1 -> x0, local copies, waits for them, and re-layouts: 1.87 us -> none
    reshape x0 -> x1, local copies, waits for them, and re-layouts: none -> 1.87 us  [fused(): return jnp.transpose(scores, (1, 0, 2)).reshape(queries, PBLK_DEV * PB)]
where the time goes in v4:
time: 46.9 us; the launch traced here: 46.8 us
  Pallas kernels  44.3 us (94%)
  local copies, waits for them, and re-layouts  1.87 us (4%)
  between operations  0.66 us (1%)
    pallas_call x1, Pallas kernels, fused(): pl.pallas_call(fused_kernel, out_shape=jax.ShapeDtypeStruct((PBLK_DEV, qu...  44.3 us
    reshape x1, local copies, waits for them, and re-layouts, fused(): return jnp.transpose(scores, (1, 0, 2)).reshape(queries, PBLK_DEV * PB)  1.87 us

profile of v4, /device:TPU:27, one launch (start us, length us, event | category | flops | bytes accessed | tf_op | source)
XLA Modules:
  0.0 46.8 jit_solution(731133839119237931)
XLA Ops:
  0.7 44.3 %encode_and_score.1 = f32[16,64,128]{2,1,0:T(8,128)} custom-call(bf16[512,256]{1,0:T(8,128)(2,1)} %hs_ref.1, bf16[1024,4096]{1,0:T(8,128)(2,1)} %w_ref.1, bf16[128,128,128]{2,1,0:T(8,128)(2,1)} %tiles_ref.1, s32[1,128]{1,0:T(1,128)} %act_hbm.1, s32[1,1]{1,0:T(1,128)} %bitcast.8.cnt_hbm, s32[1,16]{1,0:T(1,128)} %bitcast.9, s32[1,128]{1,0:T(1,128)} %pb_hbm.1), custom_call_target="tpu_custom_call" | custom-call | tf_op jit(solution)/shard_map/encode_and_score/pallas_call | solution.py:348
  44.9 1.9 %copy_bitcast_fusion = f32[64,2048]{1,0:T(8,128)} fusion(f32[16,64,128]{2,1,0:T(8,128)} %encode_and_score.1), kind=kLoop, calls=%fused_computation | loop fusion | bytes 1048576 | tf_op jit(solution)/shard_map/reshape | solution.py:388
